TPU v7x, 32 devices: a whole 2x2x4 slice. The times are simulated.
32 devices in a mesh: group: 2 (over x), seq: 2 (over y), mp: 8 (over z, core).
Axes of the slice: x: 2, y: 2, z: 4, core: 2. Of those that a mesh axis runs over, the one named last changes fastest.
Arguments:
- image_tokens: bfloat16 [256, 1280], P(('group', 'seq')), may hold values from -6 to 6
- ln_gain: float32 [1280], replicated, may hold values from 0.25 to 1.75
- ln_bias: float32 [1280], replicated, may hold values from -3 to 3
- mlp_in: bfloat16 [1280, 5120], P(None, 'mp'), may hold values from -0.15625 to 0.15625
- mlp_out: bfloat16 [5120, 1280], P('mp'), may hold values from -0.078125 to 0.078125
- key_proj: bfloat16 [1280, 1024], P(None, 'mp'), may hold values from -0.15625 to 0.15625
- value_proj: bfloat16 [1280, 1024], P(None, 'mp'), may hold values from -0.15625 to 0.15625
- text_tokens: bfloat16 [512, 4096], P(('group', 'seq')), may hold values from -6 to 6
- text_gain: float32 [4096], replicated, may hold values from 0.25 to 1.75
- query_proj: bfloat16 [4096, 4096], P('seq', 'mp'), may hold values from -0.09375 to 0.09375
- output_proj: bfloat16 [4096, 4096], P('seq', 'mp'), may hold values from -0.09375 to 0.09375
- attn_gate: float32 [1], replicated, may hold values from 0.4 to 1.2
- doc_image: int32 [4], P(('group', 'seq')), may hold values from -1 to 1
- out_cotangent: bfloat16 [512, 4096], P(('group', 'seq')), may hold values from -6 to 6
Outputs:
- text_out: bfloat16 [512, 4096], P(('group', 'seq'), 'mp')
- image_grad: float32 [256, 1280], P(('group', 'seq'))
Inputs may be any that keep to these rules, and one draw needn't show every extreme that they name: `doc_image`: entry b names the image that text tokens b * 128 to (b + 1) * 128 - 1 read; -1 means the block reads no image.
All inputs are finite; a program needn't handle non-finite values.
Results may differ from a plain program's by a relative error of at most 0.014.
Values may be sent and summed in bfloat16 or wider, within the bound.
A program may use at most 64 MiB of HBM per device.

v0:
```python
import jax
import jax.numpy as jnp
from jax import lax
from jax.sharding import PartitionSpec as P

HT = 128
BLOCK = 128


EPS_VISION = 1e-06
EPS_TEXT = 1e-05
GELU_COEF = 0.7978845608028654
CUBIC_COEF = 0.044715


def from_partner(x, axis, stride):
    return lax.ppermute(x, axis, [(i, i ^ 1 << stride) for i in range(lax.axis_size(axis))])


def gelu_parts(pre_act):
    cube_term = pre_act * pre_act * pre_act
    tangent = jnp.tanh(GELU_COEF * (pre_act + CUBIC_COEF * cube_term))
    gelu_value = 0.5 * pre_act * (1.0 + tangent)
    gelu_slope = 0.5 * (1.0 + tangent) + 0.5 * pre_act * (1.0 - tangent * tangent) * GELU_COEF * (
        1.0 + 3.0 * CUBIC_COEF * pre_act * pre_act
    )
    return (gelu_value, gelu_slope)


def layer_norm(image_tokens, ln_gain, ln_bias):
    image_float = image_tokens.astype(jnp.float32)
    centred = image_float - jnp.mean(image_float, axis=1, keepdims=True)
    inv_scale = lax.rsqrt(jnp.mean(centred * centred, axis=1, keepdims=True) + EPS_VISION)
    normed_hat = centred * inv_scale
    normed = (normed_hat * ln_gain + ln_bias).astype(jnp.bfloat16)
    return (image_float, normed_hat, inv_scale, normed)


def norm_backward(d_normed, normed_hat, inv_scale, ln_gain):
    scaled = d_normed * ln_gain
    first_mean = jnp.mean(scaled, axis=1, keepdims=True)
    second_mean = jnp.mean(scaled * normed_hat, axis=1, keepdims=True)
    return inv_scale * (scaled - first_mean - normed_hat * second_mean)


def contract_last(left, right):
    return lax.dot_general(
        left, right, (((1,), (1,)), ((), ())), preferred_element_type=jnp.float32
    )


def attend_block(queries, key_rows, value_rows, d_attended):
    head_scale = queries.shape[3] ** (-0.5)
    scores = (
        jnp.einsum("tkgd,skd->kgts", queries, key_rows, preferred_element_type=jnp.float32)
        * head_scale
    )
    top_score = jnp.max(scores, axis=3, keepdims=True)
    expo_term = jnp.exp(scores - top_score)
    soft_probs = expo_term / jnp.sum(expo_term, axis=3, keepdims=True)
    probs_half = soft_probs.astype(jnp.bfloat16)
    attended = jnp.einsum(
        "kgts,skd->tkgd", probs_half, value_rows, preferred_element_type=jnp.float32
    ).astype(jnp.bfloat16)
    delta_term = jnp.sum(d_attended.astype(jnp.float32) * attended.astype(jnp.float32), axis=3)
    d_probs = jnp.einsum(
        "tkgd,skd->kgts", d_attended, value_rows, preferred_element_type=jnp.float32
    )
    d_scores = (soft_probs * (d_probs - jnp.transpose(delta_term, (1, 2, 0))[..., None])).astype(
        jnp.bfloat16
    )
    value_grads = jnp.einsum(
        "kgts,tkgd->skd", probs_half, d_attended, preferred_element_type=jnp.float32
    )
    key_grads = (
        jnp.einsum("kgts,tkgd->skd", d_scores, queries, preferred_element_type=jnp.float32)
        * head_scale
    )
    return (attended, key_grads, value_grads)


def shards(
    image_tokens,
    ln_gain,
    ln_bias,
    mlp_in,
    mlp_out,
    key_proj,
    value_proj,
    text_tokens,
    text_gain,
    query_proj,
    output_proj,
    attn_gate,
    doc_image,
    out_cotangent,
):
    highest = lax.Precision.HIGHEST
    mp_index = lax.axis_index("mp")
    group_count = lax.axis_size("group")
    seq_count = lax.axis_size("seq")
    image_float, normed_hat, inv_scale, normed = layer_norm(image_tokens, ln_gain, ln_bias)
    pre_act = jnp.dot(normed, mlp_in, preferred_element_type=jnp.float32)
    gelu_value, gelu_slope = gelu_parts(pre_act)
    hidden_act = gelu_value.astype(jnp.bfloat16)
    mlp_term = jnp.dot(hidden_act, mlp_out, preferred_element_type=jnp.float32)
    image_state = (image_float + lax.psum(mlp_term, "mp")).astype(jnp.bfloat16)
    if key_proj.shape[1] < HT:
        partner_key, partner_value = from_partner((key_proj, value_proj), "mp", 0)
        is_odd = mp_index % 2 == 1
        key_cols = jnp.where(
            is_odd,
            jnp.concatenate([partner_key, key_proj], axis=1),
            jnp.concatenate([key_proj, partner_key], axis=1),
        )
        value_cols = jnp.where(
            is_odd,
            jnp.concatenate([partner_value, value_proj], axis=1),
            jnp.concatenate([value_proj, partner_value], axis=1),
        )
    else:
        key_cols = key_proj
        value_cols = value_proj
    kv_width = key_cols.shape[1]
    image_rows = image_tokens.shape[0]
    local_keys = jnp.dot(image_state, key_cols, preferred_element_type=jnp.float32).astype(
        jnp.bfloat16
    )
    local_values = jnp.dot(image_state, value_cols, preferred_element_type=jnp.float32).astype(
        jnp.bfloat16
    )
    key_block = local_keys.reshape(1, 1, image_rows, kv_width)
    value_block = local_values.reshape(1, 1, image_rows, kv_width)
    seq_keys, seq_values = (
        lax.all_gather(key_block, "seq", axis=1, tiled=True),
        lax.all_gather(value_block, "seq", axis=1, tiled=True),
    )
    key_grid, value_grid = (
        lax.all_gather(seq_keys, "group", axis=0, tiled=True),
        lax.all_gather(seq_values, "group", axis=0, tiled=True),
    )
    total_keys = group_count * seq_count * image_rows
    image_len = seq_count * image_rows
    kv_here = kv_width // HT
    key_all = key_grid.reshape(total_keys, kv_here, HT)
    value_all = value_grid.reshape(total_keys, kv_here, HT)
    query_full, output_full = (
        lax.all_gather(query_proj, "seq", axis=0, tiled=True),
        lax.all_gather(output_proj, "seq", axis=0, tiled=True),
    )
    text_float = text_tokens.astype(jnp.float32)
    text_scale = lax.rsqrt(jnp.mean(text_float * text_float, axis=1, keepdims=True) + EPS_TEXT)
    text_normed = (text_float * text_scale * text_gain).astype(jnp.bfloat16)
    text_rows = text_tokens.shape[0]
    block_count = text_rows // BLOCK
    heads_here = query_proj.shape[1] // HT
    group_here = heads_here // kv_here
    queries = jnp.dot(text_normed, query_full, preferred_element_type=jnp.float32).astype(
        jnp.bfloat16
    )
    queries = queries.reshape(block_count, BLOCK, kv_here, group_here, HT)
    token_doc = jnp.repeat(doc_image, BLOCK)
    has_image = (token_doc >= 0).astype(jnp.float32)[:, None]
    gate_factor = jnp.tanh(attn_gate[0])
    d_proj = (gate_factor * has_image * out_cotangent.astype(jnp.float32)).astype(jnp.bfloat16)
    d_attended = jnp.dot(d_proj, output_full, preferred_element_type=jnp.float32).astype(
        jnp.bfloat16
    )
    d_attended = d_attended.reshape(block_count, BLOCK, kv_here, group_here, HT)

    def block_step(carry, inputs):
        key_sums, value_sums = carry
        block_query, block_grad, block_doc = inputs
        chosen = jnp.maximum(block_doc, 0) * image_len
        key_rows = lax.dynamic_slice_in_dim(key_all, chosen, image_len, 0)
        value_rows = lax.dynamic_slice_in_dim(value_all, chosen, image_len, 0)
        attended, key_part, value_part = attend_block(block_query, key_rows, value_rows, block_grad)
        old_keys = lax.dynamic_slice_in_dim(key_sums, chosen, image_len, 0)
        old_values = lax.dynamic_slice_in_dim(value_sums, chosen, image_len, 0)
        key_sums = lax.dynamic_update_slice_in_dim(key_sums, old_keys + key_part, chosen, 0)
        value_sums = lax.dynamic_update_slice_in_dim(value_sums, old_values + value_part, chosen, 0)
        return ((key_sums, value_sums), attended.reshape(BLOCK, heads_here * HT))

    initial = (
        jnp.zeros((total_keys, kv_here, HT), jnp.float32),
        jnp.zeros((total_keys, kv_here, HT), jnp.float32),
    )
    (key_grads, value_grads), attended_blocks = lax.scan(
        block_step, initial, (queries, d_attended, doc_image)
    )
    attended_flat = attended_blocks.reshape(text_rows, heads_here * HT)
    text_term = contract_last(attended_flat, output_full)
    text_share = lax.psum_scatter(
        text_term.astype(jnp.bfloat16), "mp", scatter_dimension=1, tiled=True
    ).astype(jnp.float32)
    out_width = text_share.shape[1]
    text_slice = lax.dynamic_slice_in_dim(text_float, mp_index * out_width, out_width, 1)
    text_out = (text_slice + gate_factor * has_image * text_share).astype(jnp.bfloat16)
    key_pieces = key_grads.reshape(group_count, seq_count, image_rows, kv_width)
    value_pieces = value_grads.reshape(group_count, seq_count, image_rows, kv_width)
    seq_key, seq_value = (
        lax.psum_scatter(key_pieces, "seq", scatter_dimension=1, tiled=True),
        lax.psum_scatter(value_pieces, "seq", scatter_dimension=1, tiled=True),
    )
    key_back, value_back = (
        lax.psum_scatter(
            seq_key.astype(jnp.bfloat16), "group", scatter_dimension=0, tiled=True
        ).astype(jnp.float32),
        lax.psum_scatter(
            seq_value.astype(jnp.bfloat16), "group", scatter_dimension=0, tiled=True
        ).astype(jnp.float32),
    )
    key_back = key_back.reshape(image_rows, kv_width)
    value_back = value_back.reshape(image_rows, kv_width)
    state_term = jnp.dot(key_back, key_cols.astype(jnp.float32).T, precision=highest) + jnp.dot(
        value_back, value_cols.astype(jnp.float32).T, precision=highest
    )
    state_grad = lax.psum(state_term, "mp")
    d_hidden = contract_last(state_grad.astype(jnp.bfloat16), mlp_out)
    d_pre = (d_hidden * gelu_slope).astype(jnp.bfloat16)
    normed_term = contract_last(d_pre, mlp_in)
    d_normed = lax.psum(normed_term.astype(jnp.bfloat16), "mp").astype(jnp.float32)
    image_grad = state_grad + norm_backward(d_normed, normed_hat, inv_scale, ln_gain)
    return (text_out, image_grad)


def solution(mesh):
    return jax.shard_map(
        shards,
        mesh=mesh,
        in_specs=(
            P(("group", "seq"), None),
            P(),
            P(),
            P(None, "mp"),
            P("mp", None),
            P(None, "mp"),
            P(None, "mp"),
            P(("group", "seq"), None),
            P(),
            P("seq", "mp"),
            P("seq", "mp"),
            P(),
            P(("group", "seq")),
            P(("group", "seq"), None),
        ),
        out_specs=(P(("group", "seq"), "mp"), P(("group", "seq"), None)),
        check_vma=False,
    )
```

profile of v0, /device:TPU:0, one launch (start us, length us, event | category | flops | bytes accessed | tf_op | source)
XLA Modules:
  0.0 336.5 jit_solution(4227802881584980316)
XLA Ops:
  10.4 2.0 fusion.39
  17.7 54.5 %all-reduce.8.cloned.1.call-done = f32[64,1280]{1,0:T(8,128)} async-done(((f32[64,1280]{1,0:T(8,128)}), f32[64,1280]{1,0:T(8,128)}) %all-reduce.8.cloned.1.call-update) | async-done | bytes 327696 | tf_op jit(solution)/shard_map/psum | solution.py:107
  73.3 4.4 %all-gather.1 = bf16[128,128]{1,0:T(8,128)(2,1)S(1)} all-gather(bf16[64,128]{1,0:T(8,128)(2,1)S(1)} %convolution_convert_fusion.5), channel_id=3, replica_groups=mesh['group'=2,'seq'=2,'mp'=8] {'seq'}, dimensions={0}, use_global_device_ids=true | all-gather | bytes 49152 | tf_op jit(solution)/shard_map/all_gather | solution.py:135
  78.9 4.4 %all-gather = bf16[128,128]{1,0:T(8,128)(2,1)S(1)} all-gather(bf16[64,128]{1,0:T(8,128)(2,1)S(1)} %convolution_convert_fusion.6), channel_id=2, replica_groups=mesh['group'=2,'seq'=2,'mp'=8] {'seq'}, dimensions={0}, use_global_device_ids=true | all-gather | bytes 49152 | tf_op jit(solution)/shard_map/all_gather | solution.py:136
  83.4 4.6 %all_gather.21 = bf16[2,2,64,128]{3,2,1,0:T(8,128)(2,1)S(1)} all-gather(bf16[1,2,64,128]{3,2,1,0:T(8,128)(2,1)S(1)} %bitcast.145), channel_id=1, replica_groups=mesh['group'=2,'seq'=2,'mp'=8] {'group'}, dimensions={0}, use_global_device_ids=true | all-gather | bytes 98304 | tf_op jit(solution)/shard_map/all_gather | solution.py:139
  87.9 4.6 %all_gather.19 = bf16[2,2,64,128]{3,2,1,0:T(8,128)(2,1)S(1)} all-gather(bf16[1,2,64,128]{3,2,1,0:T(8,128)(2,1)S(1)} %bitcast.146), channel_id=1, replica_groups=mesh['group'=2,'seq'=2,'mp'=8] {'group'}, dimensions={0}, use_global_device_ids=true | all-gather | bytes 98304 | tf_op jit(solution)/shard_map/all_gather | solution.py:140
  92.5 3.2 convolution_convert_fusion.2
  95.9 38.0 %all-gather.5.cloned.1.call-done = bf16[4096,512]{1,0:T(8,128)(2,1)} async-done(((bf16[2048,512]{1,0:T(8,128)(2,1)}), bf16[4096,512]{1,0:T(8,128)(2,1)}) %all-gather.5.cloned.1.call-update) | async-done | bytes 4194320 | tf_op jit(solution)/shard_map/all_gather | solution.py:148
  133.9 2.9 fusion.4
  140.3 1.8 fusion.7
  142.1 11.7 %all-reduce.13 = (bf16[2,2,64,128]{3,2,1,0:T(8,128)(2,1)}, bf16[2,2,64,128]{3,2,1,0:T(8,128)(2,1)S(1)}) all-reduce(f32[2,2,64,128]{3,2,1,0:T(8,128)} %bitcast.29, f32[2,2,64,128]{3,2,1,0:T(8,128)} %bitcast.34), channel_id=5, replica_groups=mesh['group'=2,'seq'=2,'mp'=8] {'seq'}, use_global_device_ids=true, to_apply=%region_8.9.clone | all-reduce | flops 65536 | bytes 393216
  153.8 1.9 dynamic-slice_convert_fusion.1
  157.0 9.7 %reduce-scatter.12.cloned.1.call-done = bf16[1,1,64,128]{3,2,1,0:T(8,128)(2,1)} async-done(((bf16[2,1,64,128]{3,2,1,0:T(8,128)(2,1)}), bf16[1,1,64,128]{3,2,1,0:T(8,128)(2,1)}) %reduce-scatter.12.cloned.1.call-update) | async-done | bytes 16400 | tf_op jit(solution)/shard_map/reduce_scatter | solution.py:206
  166.7 2.0 fusion.89
  168.7 10.1 %reduce-scatter.14.cloned.1.call-done = bf16[1,1,64,128]{3,2,1,0:T(8,128)(2,1)} async-done(((bf16[2,1,64,128]{3,2,1,0:T(8,128)(2,1)}), bf16[1,1,64,128]{3,2,1,0:T(8,128)(2,1)}) %reduce-scatter.14.cloned.1.call-update) | async-done | bytes 16400 | tf_op jit(solution)/shard_map/reduce_scatter | solution.py:209
  178.8 2.1 convolution_add_fusion
  180.9 56.1 %all-reduce.10.cloned.1.call-done = f32[64,1280]{1,0:T(8,128)} async-done(((f32[64,1280]{1,0:T(8,128)}), f32[64,1280]{1,0:T(8,128)}) %all-reduce.10.cloned.1.call-update) | async-done | bytes 327696 | tf_op jit(solution)/shard_map/psum | solution.py:218
  237.0 2.9 convolution_convert_fusion.1
  240.0 4.8 %convolution_convert_fusion = bf16[128,4096]{1,0:T(8,128)(2,1)} fusion(bf16[128,512]{0,1:T(8,128)(2,1)} %bitcast.147, bf16[4096,512]{1,0:T(8,128)(2,1)} %all-gather.7.cloned.1.call-done), kind=kOutput, calls=%fused_computation | convolution fusion | flops 537395200 | bytes 5373952 | tf_op jit(solution)/shard_map/dot_general | solution.py:47
  244.8 1.6 convert_element_type.107
  246.4 44.7 %all-reduce.12.cloned.1.call-done = bf16[64,1280]{1,0:T(8,128)(2,1)} async-done(((bf16[64,1280]{1,0:T(8,128)(2,1)}), bf16[64,1280]{1,0:T(8,128)(2,1)}) %all-reduce.12.cloned.1.call-update) | async-done | bytes 163856 | tf_op jit(solution)/shard_map/psum | solution.py:222
  292.3 1.8 fusion.25
  294.1 33.2 %reduce-scatter.10.cloned.1.call-done = bf16[128,512]{1,0:T(8,128)(2,1)} async-done(((bf16[128,4096]{1,0:T(8,128)(2,1)}), bf16[128,512]{1,0:T(8,128)(2,1)}) %reduce-scatter.10.cloned.1.call-update) | async-done | bytes 131088 | tf_op jit(solution)/shard_map/reduce_scatter | solution.py:193
  327.3 1.7 add_convert_fusion
  (65 shorter events, 14.6 us)
Async XLA Ops:
  8.0 5.1 %copy-start = (bf16[640,1280]{1,0:T(8,128)(2,1)S(1)}, bf16[640,1280]{1,0:T(8,128)(2,1)}, u32[]{:S(2)}) copy-start(bf16[640,1280]{1,0:T(8,128)(2,1)} %param.18) | copy-start | bytes 4915204
  8.0 64.2 %all-reduce.8.cloned.1.call-start = ((), (), s32[]{:S(2)}) async-start(), calls=%async_computation.3 | async-start | bytes 655360 | tf_op jit(solution)/shard_map/psum | solution.py:107
  12.4 0.7 copy-start.5
  14.2 2.6 copy-start.13
  14.2 3.2 copy-start.3
  14.2 78.3 %all-gather.7.cloned.1.call-start = ((), (), s32[]{:S(2)}) async-start(), calls=%async_computation.5 | async-start | bytes 6291456 | tf_op jit(solution)/shard_map/all_gather | solution.py:149
  14.8 57.4 %copy-start.1 = (bf16[64,1280]{1,0:T(8,128)(2,1)S(1)}, bf16[64,1280]{1,0:T(8,128)(2,1)}, u32[]{:S(2)}) copy-start(bf16[64,1280]{1,0:T(8,128)(2,1)} %param.14) | copy-start | bytes 491524
  14.8 57.4 %copy-start.6 = (bf16[1280,128]{1,0:T(8,128)(2,1)S(1)}, bf16[1280,128]{1,0:T(8,128)(2,1)}, u32[]{:S(2)}) copy-start(bf16[1280,128]{1,0:T(8,128)(2,1)} %param.19) | copy-start | bytes 983044
  14.8 63.0 %copy-start.7 = (bf16[1280,128]{1,0:T(8,128)(2,1)S(1)}, bf16[1280,128]{1,0:T(8,128)(2,1)}, u32[]{:S(2)}) copy-start(bf16[1280,128]{1,0:T(8,128)(2,1)} %param.20) | copy-start | bytes 983044
  14.8 119.1 %all-gather.5.cloned.1.call-start = ((), (), s32[]{:S(2)}) async-start(), calls=%async_computation.4 | async-start | bytes 6291456 | tf_op jit(solution)/shard_map/all_gather | solution.py:148
  15.4 151.3 %reduce-scatter.12.cloned.1.call-start = ((), (), s32[]{:S(2)}) async-start(), calls=%async_computation.7 | async-start | bytes 49152 | tf_op jit(solution)/shard_map/reduce_scatter | solution.py:206
  92.5 41.4 %copy-start.12 = (f32[4096]{0:T(1024)S(1)}, f32[4096]{0:T(1024)}, u32[]{:S(2)}) copy-start(f32[4096]{0:T(1024)} %param.22) | copy-start | bytes 49156
  95.8 42.9 %copy-start.10 = (bf16[128,512]{1,0:T(8,128)(2,1)}, bf16[128,512]{1,0:T(8,128)(2,1)S(1)}, u32[]{:S(2)}) copy-start(bf16[128,512]{1,0:T(8,128)(2,1)S(1)} %convolution_convert_fusion.2) | copy-start | bytes 393220
  137.1 1.6 copy-start.9
  139.6 97.4 %copy-start.2 = (bf16[1280,640]{1,0:T(8,128)(2,1)S(1)}, bf16[1280,640]{1,0:T(8,128)(2,1)}, u32[]{:S(2)}) copy-start(bf16[1280,640]{1,0:T(8,128)(2,1)} %param.17) | copy-start | bytes 4915204
  155.7 23.1 %reduce-scatter.14.cloned.1.call-start = ((), (), s32[]{:S(2)}) async-start(), calls=%async_computation.8 | async-start | bytes 49152 | tf_op jit(solution)/shard_map/reduce_scatter | solution.py:209
  156.9 80.1 %all-reduce.10.cloned.1.call-start = ((), (), s32[]{:S(2)}) async-start(), calls=%async_computation.9 | async-start | bytes 655360 | tf_op jit(solution)/shard_map/psum | solution.py:218
  180.9 110.2 %all-reduce.12.cloned.1.call-start = ((), (), s32[]{:S(2)}) async-start(), calls=%async_computation.10 | async-start | bytes 327680 | tf_op jit(solution)/shard_map/psum | solution.py:222
  239.9 87.4 %reduce-scatter.10.cloned.1.call-start = ((), (), s32[]{:S(2)}) async-start(), calls=%async_computation.6 | async-start | bytes 1179648 | tf_op jit(solution)/shard_map/reduce_scatter | solution.py:193
  240.0 4.9 %copy-start.4 = (bf16[128,4096]{1,0:T(8,128)(2,1)S(1)}, bf16[128,4096]{1,0:T(8,128)(2,1)}, u32[]{:S(2)}) copy-start(bf16[128,4096]{1,0:T(8,128)(2,1)} %param.21) | copy-start | bytes 3145732
  244.8 46.3 %copy-start.11 = (f32[1280]{0:T(1024)S(1)}, f32[1280]{0:T(1024)}, u32[]{:S(2)}) copy-start(f32[1280]{0:T(1024)} %param.15) | copy-start | bytes 15364
  244.8 47.5 %copy-start.8 = (f32[64,1280]{1,0:T(8,128)S(1)}, f32[64,1280]{1,0:T(8,128)}, u32[]{:S(2)}) copy-start(f32[64,1280]{1,0:T(8,128)} %all-reduce.10.cloned.1.call-done) | copy-start | bytes 983044
Sparse Core Ops, SparseCore 0:
  14.3 57.8 all-reduce.7
  155.8 10.8 reduce-scatter.11
  169.0 9.7 reduce-scatter.13
  181.7 55.3 all-reduce.9
  240.0 51.0 all-reduce.11
  293.3 33.9 reduce-scatter.9
Sparse Core Ops, SparseCore 1:
  16.3 59.5 all-gather.6
  77.3 56.6 all-gather.4
where the time goes:
time: 337 us; the launch traced here: 336 us
  waiting for transfers between devices  248 us (74%)
  blocking collectives  29.7 us (9%)
  matrix products  27.1 us (8%)
  between operations  17.1 us (5%)
  other arithmetic  8.89 us (3%)
  local copies, waits for them, and re-layouts  5.75 us (2%)
    psum x1, waiting for transfers between devices, shards(): state_grad = lax.psum(state_term, 'mp')  56.1 us
    psum x1, waiting for transfers between devices, shards(): image_state = (image_float + lax.psum(mlp_term, 'mp')).astype(jnp.bfloat16)  54.5 us
    psum x1, waiting for transfers between devices, shards(): lax.psum(normed_term.astype(jnp.bfloat16), 'mp').astype(jnp.float32)  44.7 us
    all_gather x1, waiting for transfers between devices, shards(): lax.all_gather(query_proj, 'seq', axis=0, tiled=True)  38 us
    reduce_scatter x1, waiting for transfers between devices, shards(): lax.psum_scatter(text_term.astype(jnp.bfloat16), 'mp', scatter_dimension=...  33.2 us
    unnamed x1, blocking collectives  11.7 us
    reduce_scatter x1, waiting for transfers between devices, shards(): lax.psum_scatter(seq_value.astype(jnp.bfloat16), 'group', scatter_dimensi...  10.1 us
    reduce_scatter x1, waiting for transfers between devices, shards(): lax.psum_scatter(seq_key.astype(jnp.bfloat16), 'group', scatter_dimension...  9.72 us
  transfers between devices with their start and end apart: 8, of which 7 were waited for; matrix products, arithmetic and copies ran while one was open for 6% of the time, Pallas kernels for 0%

commit v1 on v0

--- a/solution.py
+++ b/solution.py
@@ -1,6 +1,10 @@
+import functools
+
 import jax
 import jax.numpy as jnp
 from jax import lax
+from jax.experimental import pallas as pl
+from jax.experimental.pallas import tpu as pltpu
 from jax.sharding import PartitionSpec as P
 
 HT = 128
@@ -224,9 +228,449 @@
     return (text_out, image_grad)
 
 
+def fused_kernel(
+    dims,
+    img_h, gain_ref, bias_ref, mi_h, mo_h, kp_h, vp_h, text_h, tgain_ref, wq_h, wo_h,
+    gate_ref, doc_ref, cot_h,
+    text_out, grad_out,
+    img, mi, mo, kp, vp, xt, ct, tok, wq, wo,
+    xn, dp, xr, dr, q_acc, d_acc, q_out, d_out, q_in, d_in,
+    nh_buf, inv_buf, slope_buf,
+    part1, gath1, sum1, part2, gath2, sum2, part3, gath3, sum3,
+    kv_all, gs_out, gs_in, att, t_buf, t_rcv, t_out, fin,
+    ld, bsend, brecv, ssend, srecv, rs_s, rs_r, ag_s, ag_r, kv_s, kv_r, gs_s, gs_r,
+    at_s, at_r, tb_s, tb_r, fn_s, fn_r,
+):
+    n_group, n_mp = dims
+    f32, bf16 = jnp.float32, jnp.bfloat16
+    g, s, m = lax.axis_index("group"), lax.axis_index("seq"), lax.axis_index("mp")
+    core = lax.rem(m, 2)
+    sibling = (g, s, m + 1 - 2 * core)
+    partner = (g, 1 - s, m)
+    rows, width = img.shape
+    quarter, part_cols = part1.shape[1], part1.shape[2]
+    col_parts = width // part_cols
+    text_rows, half_cols = xn.shape[1], xn.shape[2]
+    half_rows = text_rows // 2
+    n_slice = n_mp // 2
+    out_width = fin.shape[2]
+    heads = q_acc.shape[1] // HT
+    pending = []
+
+    def local(src, dst, index):
+        copy = pltpu.make_async_copy(src, dst, ld.at[index])
+        copy.start()
+        return copy
+
+    def send(src, dst, send_sem, recv_sem, device):
+        copy = pltpu.make_async_remote_copy(
+            src_ref=src, dst_ref=dst, send_sem=send_sem, recv_sem=recv_sem,
+            device_id=device, device_id_type=pl.DeviceIdType.MESH,
+        )
+        copy.start()
+        pending.append(copy)
+
+    def arrived(dst, send_sem, recv_sem, device):
+        pltpu.make_async_remote_copy(
+            src_ref=dst, dst_ref=dst, send_sem=send_sem, recv_sem=recv_sem,
+            device_id=device, device_id_type=pl.DeviceIdType.MESH,
+        ).wait_recv()
+
+    loads = {}
+    for h in range(2):
+        cols = pl.ds(h * half_cols, half_cols)
+        loads["x%d" % h] = local(text_h.at[:, cols], xt.at[h], h)
+        loads["c%d" % h] = local(cot_h.at[:, cols], ct.at[h], 2 + h)
+    loads["img"] = local(img_h, img, 4)
+    loads["mi"] = local(mi_h, mi, 5)
+    loads["mo"] = local(mo_h, mo, 6)
+    loads["wq"] = local(wq_h, wq, 7)
+    loads["wo"] = local(wo_h, wo, 8)
+    loads["kp"] = local(kp_h, kp, 9)
+    loads["vp"] = local(vp_h, vp, 10)
+    my_cols = pl.ds(pl.multiple_of(m * out_width, out_width), out_width)
+    loads["tok"] = local(text_h.at[:, my_cols], tok, 11)
+
+    mates = [(g, s, lax.rem(m + k, n_mp)) for k in range(1, n_mp)]
+    quads = [
+        (lax.rem(g + dg, n_group), lax.rem(s + ds, 2), m)
+        for dg in range(n_group)
+        for ds in range(2)
+        if dg or ds
+    ]
+    across = [(g, 1 - s, lax.rem(m + k, n_mp)) for k in range(1, n_mp)]
+    barrier = pltpu.get_barrier_semaphore()
+    greeted = mates + across + quads
+    for device in greeted:
+        pl.semaphore_signal(
+            barrier, inc=1, device_id=device, device_id_type=pl.DeviceIdType.MESH
+        )
+
+    doc = doc_ref[0]
+    has_image = jnp.where(doc >= 0, 1.0, 0.0).astype(f32)
+    gate_row = jnp.tanh(jnp.full((1, half_cols), gate_ref[0], f32)) * has_image
+
+    step = 16
+    steps = half_rows // step
+
+    def norm_rows(half):
+        def body(i, carry):
+            at = pl.ds(pl.multiple_of(half * half_rows + i * step, step), step)
+            left, right = xt[0, at].astype(f32), xt[1, at].astype(f32)
+            total = jnp.sum(left * left + right * right, axis=1, keepdims=True)
+            scale = lax.rsqrt(total / (2 * half_cols) + EPS_TEXT)
+            xn[0, at] = (left * scale * tgain_ref[:, :half_cols]).astype(bf16)
+            xn[1, at] = (right * scale * tgain_ref[:, half_cols:]).astype(bf16)
+            return carry
+
+        lax.fori_loop(0, steps, body, 0)
+
+    def grad_rows(half):
+        def body(i, carry):
+            at = pl.ds(pl.multiple_of(half * half_rows + i * step, step), step)
+            for h in range(2):
+                dp[h, at] = (gate_row * ct[h, at].astype(f32)).astype(bf16)
+            return carry
+
+        lax.fori_loop(0, steps, body, 0)
+
+    mine = pl.ds(pl.multiple_of(core * half_rows, half_rows), half_rows)
+    theirs = pl.ds(pl.multiple_of((1 - core) * half_rows, half_rows), half_rows)
+    loads["x0"].wait()
+    loads["x1"].wait()
+    norm_rows(core)
+    pl.semaphore_wait(barrier, len(greeted))
+    send(xn.at[1 - s, mine], xr.at[mine], bsend.at[0], brecv.at[0], partner)
+    loads["c0"].wait()
+    loads["c1"].wait()
+    grad_rows(core)
+    send(dp.at[1 - s, mine], dr.at[mine], bsend.at[1], brecv.at[1], partner)
+
+    def scatter(source, index, part, gath):
+        for k, device in enumerate(mates):
+            send(part.at[device[2]], gath.at[m], rs_s.at[index, k], rs_r.at[index, m], device)
+
+    def scattered(index, part, gath):
+        total = part[m].astype(f32)
+        for k, device in enumerate(mates):
+            arrived(gath.at[device[2]], rs_s.at[index, k], rs_r.at[index, device[2]], device)
+            total = total + gath[device[2]].astype(f32)
+        return total
+
+    def gather(index, sums, piece):
+        sums[m] = piece
+        for k, device in enumerate(mates):
+            send(sums.at[m], sums.at[m], ag_s.at[index, k], ag_r.at[index, m], device)
+
+    def gathered(index, sums):
+        for k, device in enumerate(mates):
+            arrived(sums.at[device[2]], ag_s.at[index, k], ag_r.at[index, device[2]], device)
+        return jnp.concatenate(
+            [
+                jnp.concatenate([sums[r * col_parts + c] for c in range(col_parts)], axis=1)
+                for r in range(rows // quarter)
+            ],
+            axis=0,
+        )
+
+    def fill(part, c, block):
+        for r in range(rows // quarter):
+            part[r * col_parts + c] = block[r * quarter : (r + 1) * quarter].astype(bf16)
+
+    loads["img"].wait()
+    image_float = img[...].astype(f32)
+    centred = image_float - jnp.mean(image_float, axis=1, keepdims=True)
+    inv_scale = lax.rsqrt(jnp.mean(centred * centred, axis=1, keepdims=True) + EPS_VISION)
+    normed_hat = centred * inv_scale
+    nh_buf[...] = normed_hat
+    inv_buf[...] = inv_scale
+    normed = (normed_hat * gain_ref[...] + bias_ref[...]).astype(bf16)
+    loads["mi"].wait()
+    pre_act = jnp.dot(normed, mi[...], preferred_element_type=f32)
+    gelu_value, gelu_slope = gelu_parts(pre_act)
+    slope_buf[...] = gelu_slope
+    hidden = gelu_value.astype(bf16)
+    loads["mo"].wait()
+    for c in range(col_parts):
+        cols = slice(c * part_cols, (c + 1) * part_cols)
+        fill(part1, c, jnp.dot(hidden, mo[:, cols], preferred_element_type=f32))
+    scatter(None, 0, part1, gath1)
+
+    norm_rows(1 - core)
+    grad_rows(1 - core)
+    loads["wq"].wait()
+    q_acc[...] = jnp.dot(xn[s], wq[...], preferred_element_type=f32)
+    loads["wo"].wait()
+    d_acc[...] = jnp.dot(dp[s], wo[...], preferred_element_type=f32)
+
+    arrived(xr.at[mine], bsend.at[0], brecv.at[0], partner)
+    send(xr.at[mine], xr.at[mine], ssend.at[0], srecv.at[0], sibling)
+
+    piece = scattered(0, part1, gath1)
+    row_at = pl.ds(pl.multiple_of(lax.div(m, col_parts) * quarter, quarter), quarter)
+    col_at = pl.ds(pl.multiple_of(lax.rem(m, col_parts) * part_cols, part_cols), part_cols)
+    gather(0, sum1, (img[row_at, col_at].astype(f32) + piece).astype(bf16))
+
+    arrived(xr.at[theirs], ssend.at[0], srecv.at[0], sibling)
+    q_out[...] = jnp.dot(xr[...], wq[...], preferred_element_type=f32).astype(bf16)
+    send(q_out, q_in, bsend.at[2], brecv.at[2], partner)
+
+    arrived(dr.at[mine], bsend.at[1], brecv.at[1], partner)
+    send(dr.at[mine], dr.at[mine], ssend.at[1], srecv.at[1], sibling)
+
+    image_state = gathered(0, sum1)
+    loads["kp"].wait()
+    loads["vp"].wait()
+    here = g * 2 + s
+    kv_all[here] = jnp.concatenate(
+        [
+            jnp.dot(image_state, kp[...], preferred_element_type=f32),
+            jnp.dot(image_state, vp[...], preferred_element_type=f32),
+        ],
+        axis=1,
+    ).astype(bf16)
+    for k, device in enumerate(quads):
+        send(kv_all.at[here], kv_all.at[here], kv_s.at[k], kv_r.at[here], device)
+
+    arrived(dr.at[theirs], ssend.at[1], srecv.at[1], sibling)
+    d_out[...] = jnp.dot(dr[...], wo[...], preferred_element_type=f32).astype(bf16)
+    send(d_out, d_in, bsend.at[3], brecv.at[3], partner)
+
+    def stacked(block):
+        return jnp.concatenate([block[:, h * HT : (h + 1) * HT] for h in range(heads)], axis=0)
+
+    def unstacked(block):
+        return jnp.concatenate(
+            [block[h * text_rows : (h + 1) * text_rows] for h in range(heads)], axis=1
+        )
+
+    head_scale = HT ** (-0.5)
+    for k, device in enumerate(quads):
+        at = device[0] * 2 + device[1]
+        arrived(kv_all.at[at], kv_s.at[k], kv_r.at[at], device)
+    chosen = jnp.maximum(doc, 0)
+    picks = [jnp.where(chosen == i, 1.0, 0.0).astype(f32) for i in range(n_group)]
+    kv = sum(
+        picks[i]
+        * jnp.concatenate([kv_all[2 * i], kv_all[2 * i + 1]], axis=0).astype(f32)
+        for i in range(n_group)
+    ).astype(bf16)
+    keys, values = kv[:, :HT], kv[:, HT:]
+    arrived(q_in, bsend.at[2], brecv.at[2], partner)
+    queries = stacked((q_acc[...] + q_in[...].astype(f32)).astype(bf16))
+    scores = contract_last(queries, keys) * head_scale
+    expo = jnp.exp(scores - jnp.max(scores, axis=1, keepdims=True))
+    soft_probs = expo / jnp.sum(expo, axis=1, keepdims=True)
+    probs_half = soft_probs.astype(bf16)
+    attended = jnp.dot(probs_half, values, preferred_element_type=f32).astype(bf16)
+    att[0] = unstacked(attended)
+    send(att.at[0], att.at[1], at_s.at[0], at_r.at[0], partner)
+
+    arrived(d_in, bsend.at[3], brecv.at[3], partner)
+    d_att = stacked((d_acc[...] + d_in[...].astype(f32)).astype(bf16))
+    delta = jnp.sum(d_att.astype(f32) * attended.astype(f32), axis=1, keepdims=True)
+    d_scores = (soft_probs * (contract_last(d_att, values) - delta)).astype(bf16)
+    first = (((0,), (0,)), ((), ()))
+    grads = jnp.concatenate(
+        [
+            lax.dot_general(d_scores, queries, first, preferred_element_type=f32) * head_scale,
+            lax.dot_general(probs_half, d_att, first, preferred_element_type=f32),
+        ],
+        axis=1,
+    )
+    for i in range(n_group):
+        for j in range(2):
+            gs_out[2 * i + j] = (picks[i] * grads[j * rows : (j + 1) * rows]).astype(bf16)
+    for k, device in enumerate(quads):
+        at = device[0] * 2 + device[1]
+        send(gs_out.at[at], gs_in.at[here], gs_s.at[k], gs_r.at[here], device)
+    back = gs_out[here].astype(f32)
+    for k, device in enumerate(quads):
+        at = device[0] * 2 + device[1]
+        arrived(gs_in.at[at], gs_s.at[k], gs_r.at[at], device)
+        back = back + gs_in[at].astype(f32)
+    back = back.astype(bf16)
+
+    for c in range(col_parts):
+        cols = slice(c * part_cols, (c + 1) * part_cols)
+        fill(
+            part2,
+            c,
+            contract_last(back[:, :HT], kp[cols, :]) + contract_last(back[:, HT:], vp[cols, :]),
+        )
+    scatter(None, 1, part2, gath2)
+
+    arrived(att.at[1], at_s.at[0], at_r.at[0], partner)
+    both = jnp.concatenate([att[0], att[1]], axis=0)
+    for j in range(n_slice):
+        term = contract_last(both, wo[j * out_width : (j + 1) * out_width, :]).astype(bf16)
+        for r in range(2):
+            for h in range(2):
+                low = r * text_rows + h * half_rows
+                t_buf[h, j, r] = term[low : low + half_rows]
+        send(t_buf.at[1 - core, j], t_rcv.at[j], tb_s.at[j], tb_r.at[j], sibling)
+
+    gather(1, sum2, scattered(1, part2, gath2).astype(bf16))
+
+    at_self = lax.div(m, n_slice) == s
+    place = s * n_slice
+
+    for j in range(n_slice):
+        arrived(t_rcv.at[j], tb_s.at[j], tb_r.at[j], sibling)
+        t_out[j] = (t_buf[core, j].astype(f32) + t_rcv[j].astype(f32)).astype(bf16)
+        send(t_out.at[j, 1], fin.at[m], fn_s.at[j, 1], fn_r.at[m], (g, 1 - s, place + j))
+        direct = pltpu.make_async_remote_copy(
+            src_ref=t_out.at[j, 0], dst_ref=fin.at[m], send_sem=fn_s.at[j, 0],
+            recv_sem=fn_r.at[m], device_id=(g, s, place + j),
+            device_id_type=pl.DeviceIdType.MESH,
+        )
+
+        @pl.when(m != place + j)
+        def _():
+            direct.start()
+
+        @pl.when(m == place + j)
+        def _():
+            fin[m] = t_out[j, 0]
+
+    state_grad = gathered(1, sum2)
+    d_hidden = contract_last(state_grad, mo[...])
+    d_pre = (d_hidden * slope_buf[...]).astype(bf16)
+    for c in range(col_parts):
+        cols = slice(c * part_cols, (c + 1) * part_cols)
+        fill(part3, c, contract_last(d_pre, mi[cols, :]))
+    scatter(None, 2, part3, gath3)
+    gather(2, sum3, scattered(2, part3, gath3).astype(bf16))
+
+    loads["tok"].wait()
+    for src in range(n_mp):
+
+        @pl.when(jnp.logical_not(jnp.logical_and(at_self, m == src)))
+        def _():
+            arrived(fin.at[src], fn_s.at[0, 0], fn_r.at[src], (g, 1 - s, src))
+
+    gate_out = gate_row[:, :out_width]
+    for h in range(2):
+        total = fin[h].astype(f32)
+        for z in range(1, n_mp // 2):
+            total = total + fin[2 * z + h].astype(f32)
+        at = slice(h * half_rows, (h + 1) * half_rows)
+        text_out[at] = (tok[at].astype(f32) + gate_out * total).astype(bf16)
+
+    d_normed = gathered(2, sum3).astype(f32)
+    grad_out[...] = gathered_state(sum2, rows, quarter, col_parts) + norm_backward(
+        d_normed, nh_buf[...], inv_buf[...], gain_ref[...]
+    )
+
+    for copy in pending:
+        copy.wait_send()
+    for j in range(n_slice):
+
+        @pl.when(m != place + j)
+        def _():
+            pltpu.make_async_remote_copy(
+                src_ref=t_out.at[j, 0], dst_ref=fin.at[m], send_sem=fn_s.at[j, 0],
+                recv_sem=fn_r.at[m], device_id=(g, s, place + j),
+                device_id_type=pl.DeviceIdType.MESH,
+            ).wait_send()
+
+
+def gathered_state(sums, rows, quarter, col_parts):
+    return jnp.concatenate(
+        [
+            jnp.concatenate([sums[r * col_parts + c] for c in range(col_parts)], axis=1)
+            for r in range(rows // quarter)
+        ],
+        axis=0,
+    ).astype(jnp.float32)
+
+
+def fused(
+    n_group, n_mp,
+    image_tokens, ln_gain, ln_bias, mlp_in, mlp_out, key_proj, value_proj,
+    text_tokens, text_gain, query_proj, output_proj, attn_gate, doc_image, out_cotangent,
+):
+    f32, bf16 = jnp.float32, jnp.bfloat16
+    rows, width = image_tokens.shape
+    hidden = mlp_in.shape[1]
+    text_rows, features = text_tokens.shape
+    head_cols = query_proj.shape[1]
+    half_cols, half_rows = features // 2, text_rows // 2
+    out_width, n_slice = features // n_mp, n_mp // 2
+    quarter = 16
+    part_cols = width // (n_mp // (rows // quarter))
+    pieces = pltpu.VMEM((n_mp, quarter, part_cols), bf16)
+    quads = 2 * n_group
+    dma = pltpu.SemaphoreType.DMA
+    hbm, vmem, smem = (
+        pl.BlockSpec(memory_space=space) for space in (pl.ANY, pltpu.VMEM, pltpu.SMEM)
+    )
+    V = pltpu.VMEM
+    scratch = [
+        V((rows, width), bf16), V(mlp_in.shape, bf16), V(mlp_out.shape, bf16),
+        V(key_proj.shape, bf16), V(value_proj.shape, bf16),
+        V((2, text_rows, half_cols), bf16), V((2, text_rows, half_cols), bf16),
+        V((text_rows, out_width), bf16),
+        V(query_proj.shape, bf16), V(output_proj.shape, bf16),
+        V((2, text_rows, half_cols), bf16), V((2, text_rows, half_cols), bf16),
+        V((text_rows, half_cols), bf16), V((text_rows, half_cols), bf16),
+        V((text_rows, head_cols), f32), V((text_rows, head_cols), f32),
+        V((text_rows, head_cols), bf16), V((text_rows, head_cols), bf16),
+        V((text_rows, head_cols), bf16), V((text_rows, head_cols), bf16),
+        V((rows, width), f32), V((rows, 1), f32), V((rows, hidden), f32),
+    ] + [pieces] * 9 + [
+        V((quads, rows, 2 * HT), bf16), V((quads, rows, 2 * HT), bf16),
+        V((quads, rows, 2 * HT), bf16),
+        V((2, text_rows, head_cols), bf16),
+        V((2, n_slice, 2, half_rows, out_width), bf16),
+        V((n_slice, 2, half_rows, out_width), bf16),
+        V((n_slice, 2, half_rows, out_width), bf16),
+        V((n_mp, half_rows, out_width), bf16),
+        dma((12,)), dma((4,)), dma((4,)), dma((2,)), dma((2,)),
+        dma((3, n_mp)), dma((3, n_mp)), dma((3, n_mp)), dma((3, n_mp)),
+        dma((quads,)), dma((quads,)), dma((quads,)), dma((quads,)),
+        dma((1,)), dma((1,)), dma((n_slice,)), dma((n_slice,)),
+        dma((n_slice, 2)), dma((n_mp,)),
+    ]
+    return pl.pallas_call(
+        functools.partial(fused_kernel, (n_group, n_mp)),
+        out_shape=(
+            jax.ShapeDtypeStruct((text_rows, out_width), bf16),
+            jax.ShapeDtypeStruct((rows, width), f32),
+        ),
+        in_specs=[hbm, vmem, vmem, hbm, hbm, hbm, hbm, hbm, vmem, hbm, hbm, smem, smem, hbm],
+        out_specs=(vmem, vmem),
+        scratch_shapes=scratch,
+        compiler_params=pltpu.CompilerParams(
+            collective_id=0, has_side_effects=True, vmem_limit_bytes=44 * 1024 * 1024
+        ),
+    )(
+        image_tokens, ln_gain.reshape(1, -1), ln_bias.reshape(1, -1), mlp_in, mlp_out,
+        key_proj, value_proj, text_tokens, text_gain.reshape(1, -1), query_proj, output_proj,
+        attn_gate, doc_image, out_cotangent,
+    )
+
+
+def fits(mesh, args):
+    n_seq, n_mp = mesh.shape["seq"], mesh.shape["mp"]
+    image_tokens, key_proj, text_tokens = args[0], args[5], args[7]
+    rows, width = image_tokens.shape
+    text_rows, features = text_tokens.shape
+    if n_seq != 2 or n_mp % 2 or key_proj.shape[1] != HT or text_rows != BLOCK:
+        return False
+    if rows % 16 or n_mp % (rows // 16) or features % (n_mp * 128):
+        return False
+    return width % (n_mp // (rows // 16) * 128) == 0
+
+
 def solution(mesh):
+    def body(*args):
+        if fits(mesh, args):
+            return fused(mesh.shape["group"], mesh.shape["mp"], *args)
+        return shards(*args)
+
     return jax.shard_map(
-        shards,
+        body,
         mesh=mesh,
         in_specs=(
             P(("group", "seq"), None),

time: 337 us -> 90.6 us (0.27)
  waiting for transfers between devices: 248 us -> 0 us
  Pallas kernels: 0 us -> 74.6 us
  blocking collectives: 29.7 us -> 0 us
  matrix products: 27.1 us -> 0 us
  between operations: 17.1 us -> 1.94 us
  other arithmetic: 8.89 us -> 0 us
  local copies, waits for them, and re-layouts: 5.75 us -> 13.3 us
    psum x3 -> x0, waiting for transfers between devices: 155 us -> none  [the longest x1 56.1 us: shards(): state_grad = lax.psum(state_term, 'mp')]
    pallas_call x0 -> x1, Pallas kernels: none -> 74.6 us  [fused(): pl.pallas_call(functools.partial(fused_kernel, (n_group, n_mp)), out_shap...]
    reduce_scatter x3 -> x0, waiting for transfers between devices: 53.1 us -> none  [the longest x1 33.2 us: shards(): lax.psum_scatter(text_term.astype(jnp.bfloat16), 'mp', scatter_dimension=...]
    all_gather x2 -> x0, waiting for transfers between devices: 38.1 us -> none  [the longest x1 38 us: shards(): lax.all_gather(query_proj, 'seq', axis=0, tiled=True)]
    dot_general x14 -> x0, matrix products: 27.1 us -> none  [the longest x2 7.69 us: contract_last(): lax.dot_general(left, right, (((1,), (1,)), ((), ())), preferred_element_...]
    all_gather x4 -> x0, blocking collectives: 18 us -> none  [the longest x1 4.58 us: shards(): lax.all_gather(seq_values, 'group', axis=0, tiled=True)]
    unnamed x1 -> x0, blocking collectives: 11.7 us -> none
    unnamed x29 -> x20, local copies, waits for them, and re-layouts: 1.28 us -> 11.9 us
  transfers between devices with their start and end apart: 8 -> 0, of which waited for: 7 -> 0; matrix products, arithmetic and copies ran while one was open for 6% -> 0% of each run, Pallas kernels for 0% -> 0%
where the time goes in v1:
time: 90.6 us; the launch traced here: 89.8 us
  Pallas kernels  74.6 us (82%)
  local copies, waits for them, and re-layouts  13.3 us (15%)
  between operations  1.94 us (2%)
    pallas_call x1, Pallas kernels, fused(): pl.pallas_call(functools.partial(fused_kernel, (n_group, n_mp)), out_shap...  74.6 us
    unnamed x20, local copies, waits for them, and re-layouts  11.9 us

profile of v1, /device:TPU:0, one launch (start us, length us, event | category | flops | bytes accessed | tf_op | source)
XLA Modules:
  0.0 89.8 jit_solution(12815110117689172060)
XLA Ops:
  1.9 0.7 reshape.13.gain_ref
  2.6 0.7 reshape.14.bias_ref
  3.3 0.0 copy-start
  3.3 1.6 %copy-done = bf16[2048,512]{1,0:T(8,128)(2,1)S(1)} copy-done((bf16[2048,512]{1,0:T(8,128)(2,1)S(1)}, bf16[2048,512]{1,0:T(8,128)(2,1)}, u32[]{:S(2)}) %copy-start) | copy-done | bytes 2097176
  4.9 0.0 copy-start.1
  4.9 1.4 %copy-done.1 = bf16[1280,640]{1,0:T(8,128)(2,1)S(1)} copy-done((bf16[1280,640]{1,0:T(8,128)(2,1)S(1)}, bf16[1280,640]{1,0:T(8,128)(2,1)}, u32[]{:S(2)}) %copy-start.1) | copy-done | bytes 1638424
  6.3 0.0 copy-start.2
  6.4 1.4 %copy-done.2 = bf16[640,1280]{1,0:T(8,128)(2,1)S(1)} copy-done((bf16[640,1280]{1,0:T(8,128)(2,1)S(1)}, bf16[640,1280]{1,0:T(8,128)(2,1)}, u32[]{:S(2)}) %copy-start.2) | copy-done | bytes 1638424
  7.8 0.0 copy-start.3
  7.8 1.2 %copy-done.3 = bf16[128,4096]{1,0:T(8,128)(2,1)S(1)} copy-done((bf16[128,4096]{1,0:T(8,128)(2,1)S(1)}, bf16[128,4096]{1,0:T(8,128)(2,1)}, u32[]{:S(2)}) %copy-start.3) | copy-done | bytes 1048600
  9.0 0.0 copy-start.4
  9.0 1.2 %copy-done.4 = bf16[128,4096]{1,0:T(8,128)(2,1)S(1)} copy-done((bf16[128,4096]{1,0:T(8,128)(2,1)S(1)}, bf16[128,4096]{1,0:T(8,128)(2,1)}, u32[]{:S(2)}) %copy-start.4) | copy-done | bytes 1048600
  10.2 0.0 copy-start.5
  10.2 1.0 %copy-done.5 = bf16[1280,128]{1,0:T(8,128)(2,1)S(1)} copy-done((bf16[1280,128]{1,0:T(8,128)(2,1)S(1)}, bf16[1280,128]{1,0:T(8,128)(2,1)}, u32[]{:S(2)}) %copy-start.5) | copy-done | bytes 327704
  11.2 0.0 copy-start.6
  11.2 1.0 %copy-done.6 = bf16[1280,128]{1,0:T(8,128)(2,1)S(1)} copy-done((bf16[1280,128]{1,0:T(8,128)(2,1)S(1)}, bf16[1280,128]{1,0:T(8,128)(2,1)}, u32[]{:S(2)}) %copy-start.6) | copy-done | bytes 327704
  12.2 0.0 copy-start.7
  12.2 0.9 %copy-done.7 = bf16[64,1280]{1,0:T(8,128)(2,1)S(1)} copy-done((bf16[64,1280]{1,0:T(8,128)(2,1)S(1)}, bf16[64,1280]{1,0:T(8,128)(2,1)}, u32[]{:S(2)}) %copy-start.7) | copy-done | bytes 163864
  13.1 0.0 copy-start.8
  13.1 0.7 copy-done.8
  13.8 74.6 %shard_map.149 = (bf16[128,512]{1,0:T(8,128)(2,1)S(1)}, f32[64,1280]{1,0:T(8,128)S(1)}) custom-call(bf16[64,1280]{1,0:T(8,128)(2,1)S(1)} %copy-done.7, f32[1,1280]{1,0:T(1,128)S(1)} %reshape.13.gain_ref, f32[1,1280]{1,0:T(1,128)S(1)} %reshape.14.bias_ref, bf16[1280,640]{1,0:T(8,128)(2,1)S(1)} %copy-done.1, bf16[640,1280]{1,0:T(8,128)(2,1)S(1)} %copy-done.2, ...), custom_call_target="tpu_custom_call" | custom-call | tf_op jit(solution)/shard_map/pallas_call | solution.py:635
  88.4 0.7 copy.20
  89.1 0.7 copy.21
Async XLA Ops:
  3.3 1.6 %copy-start = (bf16[2048,512]{1,0:T(8,128)(2,1)S(1)}, bf16[2048,512]{1,0:T(8,128)(2,1)}, u32[]{:S(2)}) copy-start(bf16[2048,512]{1,0:T(8,128)(2,1)} %wq_h.1) | copy-start | bytes 6291460
  4.9 1.4 %copy-start.1 = (bf16[1280,640]{1,0:T(8,128)(2,1)S(1)}, bf16[1280,640]{1,0:T(8,128)(2,1)}, u32[]{:S(2)}) copy-start(bf16[1280,640]{1,0:T(8,128)(2,1)} %mi_h.1) | copy-start | bytes 4915204
  6.3 1.4 %copy-start.2 = (bf16[640,1280]{1,0:T(8,128)(2,1)S(1)}, bf16[640,1280]{1,0:T(8,128)(2,1)}, u32[]{:S(2)}) copy-start(bf16[640,1280]{1,0:T(8,128)(2,1)} %mo_h.1) | copy-start | bytes 4915204
  7.8 1.2 %copy-start.3 = (bf16[128,4096]{1,0:T(8,128)(2,1)S(1)}, bf16[128,4096]{1,0:T(8,128)(2,1)}, u32[]{:S(2)}) copy-start(bf16[128,4096]{1,0:T(8,128)(2,1)} %text_h.1) | copy-start | bytes 3145732
  9.0 1.2 %copy-start.4 = (bf16[128,4096]{1,0:T(8,128)(2,1)S(1)}, bf16[128,4096]{1,0:T(8,128)(2,1)}, u32[]{:S(2)}) copy-start(bf16[128,4096]{1,0:T(8,128)(2,1)} %cot_h.1) | copy-start | bytes 3145732
  10.2 1.0 %copy-start.5 = (bf16[1280,128]{1,0:T(8,128)(2,1)S(1)}, bf16[1280,128]{1,0:T(8,128)(2,1)}, u32[]{:S(2)}) copy-start(bf16[1280,128]{1,0:T(8,128)(2,1)} %kp_h.1) | copy-start | bytes 983044
  11.2 1.0 %copy-start.6 = (bf16[1280,128]{1,0:T(8,128)(2,1)S(1)}, bf16[1280,128]{1,0:T(8,128)(2,1)}, u32[]{:S(2)}) copy-start(bf16[1280,128]{1,0:T(8,128)(2,1)} %vp_h.1) | copy-start | bytes 983044
  12.2 0.9 %copy-start.7 = (bf16[64,1280]{1,0:T(8,128)(2,1)S(1)}, bf16[64,1280]{1,0:T(8,128)(2,1)}, u32[]{:S(2)}) copy-start(bf16[64,1280]{1,0:T(8,128)(2,1)} %img_h.1) | copy-start | bytes 491524
  13.1 0.7 copy-start.8

commit v2 on v1

--- a/solution.py
+++ b/solution.py
@@ -236,10 +236,10 @@
     img, mi, mo, kp, vp, xt, ct, tok, wq, wo,
     xn, dp, xr, dr, q_acc, d_acc, q_out, d_out, q_in, d_in,
     nh_buf, inv_buf, slope_buf,
-    part1, gath1, sum1, part2, gath2, sum2, part3, gath3, sum3,
-    kv_all, gs_out, gs_in, att, t_buf, t_rcv, t_out, fin,
-    ld, bsend, brecv, ssend, srecv, rs_s, rs_r, ag_s, ag_r, kv_s, kv_r, gs_s, gs_r,
-    at_s, at_r, tb_s, tb_r, fn_s, fn_r,
+    acc, sib_out, sib_in, z_out, z_in, gath,
+    kv_all, gs_out, gs_in, att, t_buf, t_rcv, t_out, relay, fin,
+    ld, bsend, brecv, ssend, srecv, sb_s, sb_r, rs_s, rs_r, ag_s, ag_r, fw_s, fw_r, kv_s, kv_r, gs_s, gs_r,
+    at_s, at_r, tb_s, tb_r, rl_s, rl_r, fn_s, fn_r,
 ):
     n_group, n_mp = dims
     f32, bf16 = jnp.float32, jnp.bfloat16
@@ -248,14 +248,16 @@
     sibling = (g, s, m + 1 - 2 * core)
     partner = (g, 1 - s, m)
     rows, width = img.shape
-    quarter, part_cols = part1.shape[1], part1.shape[2]
-    col_parts = width // part_cols
+    chips, chip = n_mp // 2, lax.div(m, 2)
+    quarter, half_width = rows // chips, width // 2
     text_rows, half_cols = xn.shape[1], xn.shape[2]
     half_rows = text_rows // 2
     n_slice = n_mp // 2
     out_width = fin.shape[2]
     heads = q_acc.shape[1] // HT
     pending = []
+    ln_gain, ln_bias = gain_ref[...][None, :], bias_ref[...][None, :]
+    text_gain = tgain_ref[...][None, :]
 
     def local(src, dst, index):
         copy = pltpu.make_async_copy(src, dst, ld.at[index])
@@ -298,9 +300,9 @@
         for ds in range(2)
         if dg or ds
     ]
-    across = [(g, 1 - s, lax.rem(m + k, n_mp)) for k in range(1, n_mp)]
+    columns = [(g, s, lax.rem(m + 2 * k, n_mp)) for k in range(1, chips)]
     barrier = pltpu.get_barrier_semaphore()
-    greeted = mates + across + quads
+    greeted = mates + quads
     for device in greeted:
         pl.semaphore_signal(
             barrier, inc=1, device_id=device, device_id_type=pl.DeviceIdType.MESH
@@ -319,8 +321,8 @@
             left, right = xt[0, at].astype(f32), xt[1, at].astype(f32)
             total = jnp.sum(left * left + right * right, axis=1, keepdims=True)
             scale = lax.rsqrt(total / (2 * half_cols) + EPS_TEXT)
-            xn[0, at] = (left * scale * tgain_ref[:, :half_cols]).astype(bf16)
-            xn[1, at] = (right * scale * tgain_ref[:, half_cols:]).astype(bf16)
+            xn[0, at] = (left * scale * text_gain[:, :half_cols]).astype(bf16)
+            xn[1, at] = (right * scale * text_gain[:, half_cols:]).astype(bf16)
             return carry
 
         lax.fori_loop(0, steps, body, 0)
@@ -346,36 +348,54 @@
     grad_rows(core)
     send(dp.at[1 - s, mine], dr.at[mine], bsend.at[1], brecv.at[1], partner)
 
-    def scatter(source, index, part, gath):
-        for k, device in enumerate(mates):
-            send(part.at[device[2]], gath.at[m], rs_s.at[index, k], rs_r.at[index, m], device)
-
-    def scattered(index, part, gath):
-        total = part[m].astype(f32)
-        for k, device in enumerate(mates):
-            arrived(gath.at[device[2]], rs_s.at[index, k], rs_r.at[index, device[2]], device)
-            total = total + gath[device[2]].astype(f32)
+    my_half = pl.ds(pl.multiple_of(core * half_width, half_width), half_width)
+    its_half = pl.ds(pl.multiple_of((1 - core) * half_width, half_width), half_width)
+
+    def rows_of(at):
+        return pl.ds(pl.multiple_of(at * quarter, quarter), quarter)
+
+    def reduce_start(i, term):
+        sib_out[i] = term(its_half).astype(bf16)
+        send(sib_out.at[i], sib_in.at[i], sb_s.at[i], sb_r.at[i], sibling)
+        acc[...] = term(my_half)
+
+    def reduce_cross(i):
+        arrived(sib_in.at[i], sb_s.at[i], sb_r.at[i], sibling)
+        total = acc[...] + sib_in[i].astype(f32)
+        acc[...] = total
+        z_out[i] = total.astype(bf16)
+        for k, device in enumerate(columns):
+            there = lax.div(device[2], 2)
+            send(
+                z_out.at[i, rows_of(there)], z_in.at[i, chip], rs_s.at[i, k],
+                rs_r.at[i, chip], device,
+            )
+
+    def reduce_end(i):
+        total = acc[rows_of(chip)]
+        for k, device in enumerate(columns):
+            there = lax.div(device[2], 2)
+            arrived(z_in.at[i, there], rs_s.at[i, k], rs_r.at[i, there], device)
+            total = total + z_in[i, there].astype(f32)
         return total
 
-    def gather(index, sums, piece):
-        sums[m] = piece
-        for k, device in enumerate(mates):
-            send(sums.at[m], sums.at[m], ag_s.at[index, k], ag_r.at[index, m], device)
-
-    def gathered(index, sums):
-        for k, device in enumerate(mates):
-            arrived(sums.at[device[2]], ag_s.at[index, k], ag_r.at[index, device[2]], device)
-        return jnp.concatenate(
-            [
-                jnp.concatenate([sums[r * col_parts + c] for c in range(col_parts)], axis=1)
-                for r in range(rows // quarter)
-            ],
-            axis=0,
-        )
-
-    def fill(part, c, block):
-        for r in range(rows // quarter):
-            part[r * col_parts + c] = block[r * quarter : (r + 1) * quarter].astype(bf16)
+    def gather_start(i, piece):
+        gath[i, core, rows_of(chip)] = piece
+        own = gath.at[i, core, rows_of(chip)]
+        for k, device in enumerate(columns):
+            send(own, own, ag_s.at[i, k], ag_r.at[i, chip], device)
+        send(own, own, fw_s.at[i, 0], fw_r.at[i, chip], sibling)
+
+    def gather_end(i):
+        for k, device in enumerate(columns):
+            there = lax.div(device[2], 2)
+            part = gath.at[i, core, rows_of(there)]
+            arrived(part, ag_s.at[i, k], ag_r.at[i, there], device)
+            send(part, part, fw_s.at[i, k + 1], fw_r.at[i, there], sibling)
+        for there in range(chips):
+            part = gath.at[i, 1 - core, rows_of(there)]
+            arrived(part, fw_s.at[i, 0], fw_r.at[i, there], sibling)
+        return jnp.concatenate([gath[i, 0], gath[i, 1]], axis=1)
 
     loads["img"].wait()
     image_float = img[...].astype(f32)
@@ -384,19 +404,17 @@
     normed_hat = centred * inv_scale
     nh_buf[...] = normed_hat
     inv_buf[...] = inv_scale
-    normed = (normed_hat * gain_ref[...] + bias_ref[...]).astype(bf16)
+    normed = (normed_hat * ln_gain + ln_bias).astype(bf16)
     loads["mi"].wait()
     pre_act = jnp.dot(normed, mi[...], preferred_element_type=f32)
     gelu_value, gelu_slope = gelu_parts(pre_act)
     slope_buf[...] = gelu_slope
     hidden = gelu_value.astype(bf16)
     loads["mo"].wait()
-    for c in range(col_parts):
-        cols = slice(c * part_cols, (c + 1) * part_cols)
-        fill(part1, c, jnp.dot(hidden, mo[:, cols], preferred_element_type=f32))
-    scatter(None, 0, part1, gath1)
+    reduce_start(0, lambda cols: jnp.dot(hidden, mo[:, cols], preferred_element_type=f32))
 
     norm_rows(1 - core)
+    reduce_cross(0)
     grad_rows(1 - core)
     loads["wq"].wait()
     q_acc[...] = jnp.dot(xn[s], wq[...], preferred_element_type=f32)
@@ -406,10 +424,8 @@
     arrived(xr.at[mine], bsend.at[0], brecv.at[0], partner)
     send(xr.at[mine], xr.at[mine], ssend.at[0], srecv.at[0], sibling)
 
-    piece = scattered(0, part1, gath1)
-    row_at = pl.ds(pl.multiple_of(lax.div(m, col_parts) * quarter, quarter), quarter)
-    col_at = pl.ds(pl.multiple_of(lax.rem(m, col_parts) * part_cols, part_cols), part_cols)
-    gather(0, sum1, (img[row_at, col_at].astype(f32) + piece).astype(bf16))
+    piece = reduce_end(0)
+    gather_start(0, (img[rows_of(chip), my_half].astype(f32) + piece).astype(bf16))
 
     arrived(xr.at[theirs], ssend.at[0], srecv.at[0], sibling)
     q_out[...] = jnp.dot(xr[...], wq[...], preferred_element_type=f32).astype(bf16)
@@ -418,7 +434,7 @@
     arrived(dr.at[mine], bsend.at[1], brecv.at[1], partner)
     send(dr.at[mine], dr.at[mine], ssend.at[1], srecv.at[1], sibling)
 
-    image_state = gathered(0, sum1)
+    image_state = gather_end(0)
     loads["kp"].wait()
     loads["vp"].wait()
     here = g * 2 + s
@@ -484,6 +500,41 @@
     for k, device in enumerate(quads):
         at = device[0] * 2 + device[1]
         send(gs_out.at[at], gs_in.at[here], gs_s.at[k], gs_r.at[here], device)
+
+    def out_terms(r):
+        for j in range(n_slice):
+            term = contract_last(att[r], wo[j * out_width : (j + 1) * out_width, :]).astype(bf16)
+            for h in range(2):
+                t_buf[r, j, h] = term[h * half_rows : (h + 1) * half_rows]
+            send(
+                t_buf.at[r, j, 1 - core], t_rcv.at[r, j], tb_s.at[r, j], tb_r.at[r, j], sibling
+            )
+
+    def out_sum(r, j):
+        arrived(t_rcv.at[r, j], tb_s.at[r, j], tb_r.at[r, j], sibling)
+        t_out[r, j] = (t_buf[r, j, core].astype(f32) + t_rcv[r, j].astype(f32)).astype(bf16)
+
+    def out_copy(src, r, j):
+        return pltpu.make_async_remote_copy(
+            src_ref=src, dst_ref=fin.at[m], send_sem=fn_s.at[r, j], recv_sem=fn_r.at[m],
+            device_id=(g, s, owner(r, j)), device_id_type=pl.DeviceIdType.MESH,
+        )
+
+    def owner(r, j):
+        return (s if r == 0 else 1 - s) * n_slice + j
+
+    def out_send(src, r, j):
+        @pl.when(m != owner(r, j))
+        def _():
+            out_copy(src, r, j).start()
+
+        @pl.when(m == owner(r, j))
+        def _():
+            fin[m] = src[...]
+
+    arrived(att.at[1], at_s.at[0], at_r.at[0], partner)
+    out_terms(1)
+
     back = gs_out[here].astype(f32)
     for k, device in enumerate(quads):
         at = device[0] * 2 + device[1]
@@ -491,98 +542,53 @@
         back = back + gs_in[at].astype(f32)
     back = back.astype(bf16)
 
-    for c in range(col_parts):
-        cols = slice(c * part_cols, (c + 1) * part_cols)
-        fill(
-            part2,
-            c,
-            contract_last(back[:, :HT], kp[cols, :]) + contract_last(back[:, HT:], vp[cols, :]),
-        )
-    scatter(None, 1, part2, gath2)
-
-    arrived(att.at[1], at_s.at[0], at_r.at[0], partner)
-    both = jnp.concatenate([att[0], att[1]], axis=0)
+    reduce_start(
+        1,
+        lambda cols: contract_last(back[:, :HT], kp[cols, :])
+        + contract_last(back[:, HT:], vp[cols, :]),
+    )
     for j in range(n_slice):
-        term = contract_last(both, wo[j * out_width : (j + 1) * out_width, :]).astype(bf16)
-        for r in range(2):
-            for h in range(2):
-                low = r * text_rows + h * half_rows
-                t_buf[h, j, r] = term[low : low + half_rows]
-        send(t_buf.at[1 - core, j], t_rcv.at[j], tb_s.at[j], tb_r.at[j], sibling)
-
-    gather(1, sum2, scattered(1, part2, gath2).astype(bf16))
-
-    at_self = lax.div(m, n_slice) == s
-    place = s * n_slice
-
-    for j in range(n_slice):
-        arrived(t_rcv.at[j], tb_s.at[j], tb_r.at[j], sibling)
-        t_out[j] = (t_buf[core, j].astype(f32) + t_rcv[j].astype(f32)).astype(bf16)
-        send(t_out.at[j, 1], fin.at[m], fn_s.at[j, 1], fn_r.at[m], (g, 1 - s, place + j))
-        direct = pltpu.make_async_remote_copy(
-            src_ref=t_out.at[j, 0], dst_ref=fin.at[m], send_sem=fn_s.at[j, 0],
-            recv_sem=fn_r.at[m], device_id=(g, s, place + j),
-            device_id_type=pl.DeviceIdType.MESH,
-        )
-
-        @pl.when(m != place + j)
-        def _():
-            direct.start()
-
-        @pl.when(m == place + j)
-        def _():
-            fin[m] = t_out[j, 0]
-
-    state_grad = gathered(1, sum2)
+        out_sum(1, j)
+        send(t_out.at[1, j], relay.at[j], rl_s.at[j], rl_r.at[j], partner)
+    reduce_cross(1)
+    out_terms(0)
+    gather_start(1, reduce_end(1).astype(bf16))
+
+    state_grad = gather_end(1)
     d_hidden = contract_last(state_grad, mo[...])
     d_pre = (d_hidden * slope_buf[...]).astype(bf16)
-    for c in range(col_parts):
-        cols = slice(c * part_cols, (c + 1) * part_cols)
-        fill(part3, c, contract_last(d_pre, mi[cols, :]))
-    scatter(None, 2, part3, gath3)
-    gather(2, sum3, scattered(2, part3, gath3).astype(bf16))
+    reduce_start(2, lambda cols: contract_last(d_pre, mi[cols, :]))
+    reduce_cross(2)
+    gather_start(2, reduce_end(2).astype(bf16))
+    for j in range(n_slice):
+        out_sum(0, j)
+        out_send(t_out.at[0, j], 0, j)
+    for j in range(n_slice):
+        arrived(relay.at[j], rl_s.at[j], rl_r.at[j], partner)
+        out_send(relay.at[j], 1, j)
+    d_normed = gather_end(2).astype(f32)
+    state_grad = jnp.concatenate([gath[1, 0], gath[1, 1]], axis=1).astype(f32)
+    grad_out[...] = state_grad + norm_backward(d_normed, nh_buf[...], inv_buf[...], ln_gain)
 
     loads["tok"].wait()
-    for src in range(n_mp):
-
-        @pl.when(jnp.logical_not(jnp.logical_and(at_self, m == src)))
-        def _():
-            arrived(fin.at[src], fn_s.at[0, 0], fn_r.at[src], (g, 1 - s, src))
-
+    for k, device in enumerate(mates):
+        arrived(fin.at[device[2]], fn_s.at[0, 0], fn_r.at[device[2]], device)
     gate_out = gate_row[:, :out_width]
     for h in range(2):
         total = fin[h].astype(f32)
-        for z in range(1, n_mp // 2):
-            total = total + fin[2 * z + h].astype(f32)
+        for at in range(1, chips):
+            total = total + fin[2 * at + h].astype(f32)
         at = slice(h * half_rows, (h + 1) * half_rows)
         text_out[at] = (tok[at].astype(f32) + gate_out * total).astype(bf16)
-
-    d_normed = gathered(2, sum3).astype(f32)
-    grad_out[...] = gathered_state(sum2, rows, quarter, col_parts) + norm_backward(
-        d_normed, nh_buf[...], inv_buf[...], gain_ref[...]
-    )
 
     for copy in pending:
         copy.wait_send()
     for j in range(n_slice):
-
-        @pl.when(m != place + j)
-        def _():
-            pltpu.make_async_remote_copy(
-                src_ref=t_out.at[j, 0], dst_ref=fin.at[m], send_sem=fn_s.at[j, 0],
-                recv_sem=fn_r.at[m], device_id=(g, s, place + j),
-                device_id_type=pl.DeviceIdType.MESH,
-            ).wait_send()
-
-
-def gathered_state(sums, rows, quarter, col_parts):
-    return jnp.concatenate(
-        [
-            jnp.concatenate([sums[r * col_parts + c] for c in range(col_parts)], axis=1)
-            for r in range(rows // quarter)
-        ],
-        axis=0,
-    ).astype(jnp.float32)
+        for r, src in enumerate((t_out.at[0, j], relay.at[j])):
+
+            @pl.when(m != owner(r, j))
+            def _():
+                out_copy(src, r, j).wait_send()
 
 
 def fused(
@@ -597,9 +603,8 @@
     head_cols = query_proj.shape[1]
     half_cols, half_rows = features // 2, text_rows // 2
     out_width, n_slice = features // n_mp, n_mp // 2
-    quarter = 16
-    part_cols = width // (n_mp // (rows // quarter))
-    pieces = pltpu.VMEM((n_mp, quarter, part_cols), bf16)
+    chips, half_width = n_mp // 2, width // 2
+    halves = pltpu.VMEM((3, rows, half_width), bf16)
     quads = 2 * n_group
     dma = pltpu.SemaphoreType.DMA
     hbm, vmem, smem = (
@@ -618,19 +623,22 @@
         V((text_rows, head_cols), bf16), V((text_rows, head_cols), bf16),
         V((text_rows, head_cols), bf16), V((text_rows, head_cols), bf16),
         V((rows, width), f32), V((rows, 1), f32), V((rows, hidden), f32),
-    ] + [pieces] * 9 + [
+        V((rows, half_width), f32), halves, halves, halves,
+        V((3, chips, rows // chips, half_width), bf16), V((3, 2, rows, half_width), bf16),
         V((quads, rows, 2 * HT), bf16), V((quads, rows, 2 * HT), bf16),
         V((quads, rows, 2 * HT), bf16),
         V((2, text_rows, head_cols), bf16),
         V((2, n_slice, 2, half_rows, out_width), bf16),
-        V((n_slice, 2, half_rows, out_width), bf16),
-        V((n_slice, 2, half_rows, out_width), bf16),
+        V((2, n_slice, half_rows, out_width), bf16),
+        V((2, n_slice, half_rows, out_width), bf16),
+        V((n_slice, half_rows, out_width), bf16),
         V((n_mp, half_rows, out_width), bf16),
         dma((12,)), dma((4,)), dma((4,)), dma((2,)), dma((2,)),
-        dma((3, n_mp)), dma((3, n_mp)), dma((3, n_mp)), dma((3, n_mp)),
+        dma((3,)), dma((3,)), dma((3, chips)), dma((3, chips)), dma((3, chips)), dma((3, chips)),
+        dma((3, chips)), dma((3, chips)),
         dma((quads,)), dma((quads,)), dma((quads,)), dma((quads,)),
-        dma((1,)), dma((1,)), dma((n_slice,)), dma((n_slice,)),
-        dma((n_slice, 2)), dma((n_mp,)),
+        dma((1,)), dma((1,)), dma((2, n_slice)), dma((2, n_slice)),
+        dma((n_slice,)), dma((n_slice,)), dma((2, n_slice)), dma((n_mp,)),
     ]
     return pl.pallas_call(
         functools.partial(fused_kernel, (n_group, n_mp)),
@@ -642,11 +650,11 @@
         out_specs=(vmem, vmem),
         scratch_shapes=scratch,
         compiler_params=pltpu.CompilerParams(
-            collective_id=0, has_side_effects=True, vmem_limit_bytes=44 * 1024 * 1024
+            collective_id=0, has_side_effects=True, vmem_limit_bytes=60 * 1024 * 1024
         ),
     )(
-        image_tokens, ln_gain.reshape(1, -1), ln_bias.reshape(1, -1), mlp_in, mlp_out,
-        key_proj, value_proj, text_tokens, text_gain.reshape(1, -1), query_proj, output_proj,
+        image_tokens, ln_gain, ln_bias, mlp_in, mlp_out,
+        key_proj, value_proj, text_tokens, text_gain, query_proj, output_proj,
         attn_gate, doc_image, out_cotangent,
     )
 
@@ -658,9 +666,7 @@
     text_rows, features = text_tokens.shape
     if n_seq != 2 or n_mp % 2 or key_proj.shape[1] != HT or text_rows != BLOCK:
         return False
-    if rows % 16 or n_mp % (rows // 16) or features % (n_mp * 128):
-        return False
-    return width % (n_mp // (rows // 16) * 128) == 0
+    return rows == 8 * n_mp and features % (n_mp * 128) == 0 and width % 256 == 0
 
 
 def solution(mesh):

time: 90.6 us -> 67.8 us (0.75)
  Pallas kernels: 74.6 us -> 61.5 us
  local copies, waits for them, and re-layouts: 13.3 us -> 3.29 us
    pallas_call x1, Pallas kernels: 74.6 us -> 61.5 us  [fused(): pl.pallas_call(functools.partial(fused_kernel, (n_group, n_mp)), out_shap...]
    unnamed x20 -> x2, local copies, waits for them, and re-layouts: 11.9 us -> 3.29 us
    reshape x2 -> x0, local copies, waits for them, and re-layouts: 1.4 us -> none  [the longest x1 0.7 us: fused(): ln_gain.reshape(1, -1)]
where the time goes in v2:
time: 67.8 us; the launch traced here: 66.7 us
  Pallas kernels  61.5 us (91%)
  local copies, waits for them, and re-layouts  3.29 us (5%)
  between operations  1.93 us (3%)
    pallas_call x1, Pallas kernels, fused(): pl.pallas_call(functools.partial(fused_kernel, (n_group, n_mp)), out_shap...  61.5 us
    unnamed x2, local copies, waits for them, and re-layouts  3.29 us

profile of v2, /device:TPU:0, one launch (start us, length us, event | category | flops | bytes accessed | tf_op | source)
XLA Modules:
  0.0 66.7 jit_solution(1056244740405743331)
XLA Ops:
  1.9 61.5 %shard_map.149 = (bf16[128,512]{1,0:T(8,128)(2,1)}, f32[64,1280]{1,0:T(8,128)}) custom-call(bf16[64,1280]{1,0:T(8,128)(2,1)} %img_h.1, f32[1280]{0:T(1024)} %gain_ref.1, f32[1280]{0:T(1024)} %bias_ref.1, bf16[1280,640]{1,0:T(8,128)(2,1)} %mi_h.1, bf16[640,1280]{1,0:T(8,128)(2,1)} %mo_h.1, bf16[1280,128]{1,0:T(8,128)(2,1)} %kp_h.1, bf16[1280,128]{1,0:T(8,128)(2,1)} %vp_h.1, ...), custom_call_target="tpu_custom_call" | custom-call | tf_op jit(solution)/shard_map/pallas_call | solution.py:643
  63.4 1.6 %copy.20 = bf16[128,512]{1,0:T(8,128)(2,1)} copy(bf16[128,512]{1,0:T(8,128)(2,1)} %get-tuple-element.4) | data formatting | bytes 262144
  65.0 1.7 %copy.21 = f32[64,1280]{1,0:T(8,128)} copy(f32[64,1280]{1,0:T(8,128)} %get-tuple-element.5) | data formatting | bytes 655360
